TPU v7x, 128 devices: a whole 4x4x4 slice. The times are simulated.
128 devices in a mesh: ctx: 8 (over x_hi, z), tp: 8 (over y, x_lo), dp: 2 (over core).
Axes of the slice: x: 4 (x_hi: 2, x_lo: 2; x = x_hi * 2 + x_lo), y: 4, z: 4, core: 2. Of those that a mesh axis runs over, the one named last changes fastest.
Arguments:
- patches: bfloat16 [2, 4096, 1280], P('dp', 'ctx'), may hold values from -6 to 6
- window_ids: int32 [2, 4096], P('dp', 'ctx'), may hold values from 0 to 8191, as said below
- vit_gain: float32 [1280], replicated, may hold values from 0.1 to 1.9
- vit_qkv: bfloat16 [1280, 3, 1280], P(None, None, 'tp')
- vit_out: bfloat16 [1280, 1280], P('tp')
- merge_gain: float32 [1280], replicated, may hold values from 0.1 to 1.9
- merge_up: bfloat16 [5120, 5120], P(None, 'tp'), may hold values from -0.078125 to 0.078125
- merge_down: bfloat16 [5120, 8192], P('tp', ('ctx', 'dp')), may hold values from -0.078125 to 0.078125
- text_rows: bfloat16 [2, 4096, 8192], P('dp', 'ctx', 'tp'), may hold values from -6 to 6
- placeholders: int32 [2, 1024], P('dp', 'ctx'), may hold values from 0 to 4095, as said below
- segments: int32 [2, 4096], P('dp'), may hold values from 0 to 3, never falling along the last dimension, each value on 1 to 2048 neighbouring positions
- llm_gain: float32 [8192], replicated, may hold values from 0.1 to 1.9
- w_query: bfloat16 [8192, 4096], P(None, 'tp')
- w_keyval: bfloat16 [8192, 2, 1024], P(None, None, 'tp')
Outputs:
- attended: bfloat16 [2, 4096, 4096], P('dp', 'ctx', 'tp')
Inputs may be any that keep to these rules, and one draw needn't show every extreme that they name: `window_ids`: ids never fall along a sample's patches; a window holds 1 to 112 consecutive patches and never crosses from one ctx index's 512 patches to the next; every such block of patches holds a window of exactly 112. `placeholders`: the positions of one sample are distinct. The 128 vision rows of one ctx index put at most 32 rows into the 512 positions of any one ctx index, and exactly 32 into one of them.
All inputs are finite; a program needn't handle non-finite values.
Results may differ from a plain program's by a relative error of at most 0.025.
Values may be sent and summed in bfloat16 or wider, within the bound.
A program may use at most 128 MiB of HBM per device.

v0:
```python
import jax
import jax.numpy as jnp
from jax import lax
from jax.sharding import PartitionSpec as P

VHD = 80
HD = 128


epsilon = 1e-06
masked = -1e30


def rms_norm(values, gain):
    values = values.astype(jnp.float32)
    return values * lax.rsqrt(jnp.mean(values * values, axis=-1, keepdims=True) + epsilon) * gain


def shards(
    patches,
    window_ids,
    vit_gain,
    vit_qkv,
    vit_out,
    merge_gain,
    merge_up,
    merge_down,
    text_rows,
    placeholders,
    segments,
    llm_gain,
    w_query,
    w_keyval,
):
    own_patches = patches[0]
    window_of = window_ids[0]
    row_count = own_patches.shape[0]
    vit_heads = vit_qkv.shape[2] // VHD
    normed = rms_norm(own_patches, vit_gain).astype(jnp.bfloat16)
    projected = jnp.dot(
        normed, vit_qkv.reshape(vit_qkv.shape[0], -1), preferred_element_type=jnp.float32
    ).astype(jnp.bfloat16)
    projected = projected.reshape(row_count, 3, vit_heads, VHD)
    queries = projected[:, 0]
    key_rows = projected[:, 1]
    value_rows = projected[:, 2]
    block_rows = min(512, row_count)

    def window_block(first_row):
        scores = jnp.einsum(
            "qhd,khd->hqk", queries, key_rows, preferred_element_type=jnp.float32
        ) * VHD ** (-0.5)
        same = (window_of[:, None] == window_of[None, :])[None]
        highest = jnp.max(jnp.where(same, scores, masked), axis=-1, keepdims=True)
        weights = jnp.where(same, jnp.exp(scores - highest), 0.0)
        totals = jnp.sum(weights, axis=-1, keepdims=True)
        mixed_heads = (
            jnp.einsum(
                "hqk,khd->hqd",
                weights.astype(jnp.bfloat16),
                value_rows,
                preferred_element_type=jnp.float32,
            )
            / totals
        )
        return (
            mixed_heads.transpose(1, 0, 2).reshape(block_rows, vit_heads * VHD).astype(jnp.bfloat16)
        )

    block_starts = jnp.arange(row_count // block_rows, dtype=jnp.int32) * block_rows
    head_rows = lax.map(window_block, block_starts).reshape(row_count, vit_heads * VHD)
    partial_out = jnp.dot(head_rows, vit_out, preferred_element_type=jnp.float32)
    residual = own_patches.astype(jnp.float32) + lax.psum(partial_out, "tp")
    merged = (
        rms_norm(residual, merge_gain)
        .astype(jnp.bfloat16)
        .reshape(row_count // 4, 4 * residual.shape[1])
    )
    inner = jax.nn.gelu(
        jnp.dot(merged, merge_up, preferred_element_type=jnp.float32), approximate=False
    ).astype(jnp.bfloat16)
    terms = jnp.dot(
        inner,
        lax.all_gather(merge_down, ("ctx", "dp"), axis=1, tiled=True),
        preferred_element_type=jnp.float32,
    )
    vision = lax.psum_scatter(terms, "tp", scatter_dimension=1, tiled=True).astype(jnp.bfloat16)
    ctx_count = lax.axis_size("ctx")
    own_index = lax.axis_index("ctx")
    tok_rows = text_rows.shape[1]
    merged_count = vision.shape[0]
    capacity = 2 * (merged_count // ctx_count)
    dest_pos = placeholders[0]
    target = dest_pos // tok_rows
    dest_hit = (target[:, None] == jnp.arange(ctx_count, dtype=jnp.int32)[None, :]).astype(
        jnp.int32
    )
    earlier = jnp.cumsum(dest_hit, axis=0) - dest_hit
    rank = jnp.sum(earlier * dest_hit, axis=1)
    slot = target * capacity + rank
    slot_pick = slot[:, None] == jnp.arange(ctx_count * capacity, dtype=jnp.int32)[None, :]
    outgoing = jnp.einsum(
        "ms,mf->sf", slot_pick.astype(jnp.bfloat16), vision, preferred_element_type=jnp.float32
    ).astype(jnp.bfloat16)
    outgoing_pos = jnp.max(jnp.where(slot_pick, dest_pos[:, None], -1), axis=0)
    incoming, incoming_pos = (
        lax.all_to_all(outgoing, "ctx", split_axis=0, concat_axis=0, tiled=True),
        lax.all_to_all(outgoing_pos, "ctx", split_axis=0, concat_axis=0, tiled=True),
    )
    local_pos = incoming_pos - own_index * tok_rows
    placement = jnp.arange(tok_rows, dtype=jnp.int32)[:, None] == local_pos[None, :]
    placed = jnp.einsum(
        "ts,sf->tf", placement.astype(jnp.bfloat16), incoming, preferred_element_type=jnp.float32
    ).astype(jnp.bfloat16)
    is_vision = jnp.any(placement, axis=1)
    mixed = jnp.where(is_vision[:, None], placed, text_rows[0])
    full_rows = lax.all_gather(mixed, "tp", axis=1, tiled=True)
    llm_normed = rms_norm(full_rows, llm_gain).astype(jnp.bfloat16)
    kv_heads = w_keyval.shape[2] // HD
    per_group = w_query.shape[1] // (HD * kv_heads)
    llm_queries = jnp.dot(llm_normed, w_query, preferred_element_type=jnp.float32).astype(
        jnp.bfloat16
    )
    llm_queries = llm_queries.reshape(tok_rows, kv_heads, per_group, HD)
    keyvals = jnp.dot(
        llm_normed, w_keyval.reshape(w_keyval.shape[0], -1), preferred_element_type=jnp.float32
    ).astype(jnp.bfloat16)
    segment_ids = segments[0]
    query_pos = own_index * tok_rows + jnp.arange(tok_rows, dtype=jnp.int32)
    query_seg = lax.dynamic_slice_in_dim(segment_ids, own_index * tok_rows, tok_rows, 0)
    shard_block = lax.all_gather(keyvals, "ctx", axis=0, tiled=True)
    running_max = jnp.full((kv_heads, per_group, tok_rows), masked, jnp.float32)
    block_len = shard_block.shape[0]
    block_keys = shard_block[:, : kv_heads * HD].reshape(block_len, kv_heads, HD)
    block_values = shard_block[:, kv_heads * HD :].reshape(block_len, kv_heads, HD)
    key_pos = jnp.arange(block_len, dtype=jnp.int32)
    allowed = (query_seg[:, None] == segment_ids[None, :]) & (
        key_pos[None, :] <= query_pos[:, None]
    )
    scores = jnp.einsum(
        "qgid,kgd->giqk", llm_queries, block_keys, preferred_element_type=jnp.float32
    ) * HD ** (-0.5)
    block_max = jnp.max(jnp.where(allowed[None, None], scores, masked), axis=-1)
    new_max = jnp.maximum(running_max, block_max)
    weights = jnp.where(allowed[None, None], jnp.exp(scores - new_max[..., None]), 0.0)
    new_sum = jnp.sum(weights, axis=-1)
    new_acc = jnp.einsum(
        "giqk,kgd->giqd",
        weights.astype(jnp.bfloat16),
        block_values,
        preferred_element_type=jnp.float32,
    )
    result = new_acc / new_sum[..., None]
    result = (
        result.transpose(2, 0, 1, 3)
        .reshape(tok_rows, kv_heads * per_group * HD)
        .astype(jnp.bfloat16)
    )
    return result[None]


def solution(mesh):
    in_specs = (
        P("dp", "ctx", None),
        P("dp", "ctx"),
        P(),
        P(None, None, "tp"),
        P("tp", None),
        P(),
        P(None, "tp"),
        P("tp", ("ctx", "dp")),
        P("dp", "ctx", "tp"),
        P("dp", "ctx"),
        P("dp", None),
        P(),
        P(None, "tp"),
        P(None, None, "tp"),
    )
    out_specs = P("dp", "ctx", "tp")
    return jax.shard_map(shards, mesh=mesh, in_specs=in_specs, out_specs=out_specs, check_vma=False)
```

profile of v0, /device:TPU:96, one launch (start us, length us, event | category | flops | bytes accessed | tf_op | source)
XLA Modules:
  0.0 596.0 jit_solution(14989129940485247104)
XLA Ops:
  7.4 1.7 fusion.19
  10.8 2.2 fusion.38
  14.3 2.5 fusion.149
  16.9 2.2 fusion.47
  19.1 2.0 fusion.152
  21.8 160.0 %all-reduce.2.cloned.1.call-done = f32[512,1280]{1,0:T(8,128)} async-done(((f32[512,1280]{1,0:T(8,128)}), f32[512,1280]{1,0:T(8,128)}) %all-reduce.2.cloned.1.call-update) | async-done | bytes 2621456 | tf_op jit(solution)/shard_map/psum | solution.py:73
  181.8 2.3 multiply_reduce_fusion
  185.8 2.5 reshape.253
  188.3 11.5 %fusion.74 = f32[128,8192]{1,0:T(8,128)} fusion(bf16[640,8192]{1,0:T(8,128)(2,1)} %all-gather.4.cloned.1.call-done, bf16[128,5120]{1,0:T(8,128)(2,1)S(1)} %reshape.253, bf16[5120,640]{1,0:T(8,128)(2,1)} %param.20), kind=kOutput, calls=%fused_computation.81 | convolution fusion | flops 2186362880 | bytes 22544384 | tf_op jit(solution)/shard_map/dot_general | solution.py:82
  201.8 6.8 %all-to-all-start = ((s32[8,32,1]{1,2,0:T(1,128)}), s32[8,32,1]{1,2,0:T(1,128)S(1)}, u32[]{:S(2)}, u32[]{:S(2)}) async-start(s32[8,32,1]{1,2,0:T(1,128)} %bitcast.3), calls=%async_computation | async-start | bytes 8192 | tf_op jit(solution)/shard_map/all_to_all | solution.py:108
  208.6 82.1 %reduce-scatter.2.cloned.1.call-done = f32[128,1024]{1,0:T(8,128)} async-done(((f32[128,8192]{1,0:T(8,128)}), f32[128,1024]{1,0:T(8,128)}) %reduce-scatter.2.cloned.1.call-update) | async-done | bytes 524304 | tf_op jit(solution)/shard_map/reduce_scatter | solution.py:87
  290.7 2.2 convolution_convert_fusion.1
  292.9 6.8 %all-to-all-start.1 = ((bf16[8,32,1024]{2,1,0:T(8,128)(2,1)}), bf16[8,32,1024]{2,1,0:T(8,128)(2,1)S(1)}, u32[]{:S(2)}, u32[]{:S(2)}) async-start(bf16[8,32,1024]{2,1,0:T(8,128)(2,1)} %bitcast.15), calls=%async_computation.2 | async-start | bytes 1048576 | tf_op jit(solution)/shard_map/all_to_all | solution.py:107
  300.0 8.5 %all-to-all-done.1 = bf16[8,32,1024]{2,1,0:T(8,128)(2,1)S(1)} async-done(((bf16[8,32,1024]{2,1,0:T(8,128)(2,1)}), bf16[8,32,1024]{2,1,0:T(8,128)(2,1)S(1)}, u32[]{:S(2)}, u32[]{:S(2)}) %all-to-all-start.1) | async-done | bytes 524320 | tf_op jit(solution)/shard_map/all_to_all | solution.py:107
  310.4 167.0 %all-gather.6.cloned.1.call-done = bf16[512,8192]{1,0:T(8,128)(2,1)} async-done(((bf16[512,1024]{1,0:T(8,128)(2,1)}), bf16[512,8192]{1,0:T(8,128)(2,1)}) %all-gather.6.cloned.1.call-update) | async-done | bytes 8388624 | tf_op jit(solution)/shard_map/all_gather | solution.py:117
  477.4 5.3 fusion.6
  483.1 5.5 fusion.41
  488.7 2.2 fusion.13
  490.9 10.4 %fusion.35 = bf16[512,512]{0,1:T(8,128)(2,1)S(1)} fusion(bf16[8192,512]{1,0:T(8,128)(2,1)} %param.26, bf16[512,8192]{1,0:T(8,128)(2,1)} %all-gather.6.cloned.1.call-done, f32[8192]{0:T(1024)S(1)} %copy-done.11, f32[512]{0:T(512)S(1)} %add_rsqrt_fusion), kind=kOutput, calls=%fused_computation.42 | convolution fusion | flops 4312006656 | bytes 17336320 | tf_op jit(solution)/shard_map/dot_general | solution.py:121
  501.3 40.7 %all-gather.8.cloned.1.call-done = bf16[4096,256]{1,0:T(8,128)(2,1)} async-done(((bf16[512,256]{1,0:T(8,128)(2,1)}), bf16[4096,256]{1,0:T(8,128)(2,1)}) %all-gather.8.cloned.1.call-update) | async-done | bytes 2097168 | tf_op jit(solution)/shard_map/all_gather | solution.py:131
  542.0 14.9 %fusion.1 = (f32[4,512]{1,0:T(4,128)S(1)}, f32[4096,512,4]{1,0,2:T(8,128)}) fusion(pred[512,4096]{0,1:T(8,128)(4,1)S(1)} %fusion.13, bf16[512,4,128]{0,2,1:T(8,128)(2,1)S(1)} %bitcast.130, bf16[4096,256]{1,0:T(8,128)(2,1)} %all-gather.8.cloned.1.call-done), kind=kOutput, calls=%fused_computation.3 | convolution fusion | flops 2172647424 | bytes 37232640 | tf_op jit(solution)/shard_map/qgid,kgd->giqk/dot_general | solution.py:140
  556.9 14.5 %fusion.4 = f32[4,512]{1,0:T(4,128)S(1)} fusion(f32[4096,512,4]{1,0,2:T(8,128)} %get-tuple-element.16, f32[4,512]{1,0:T(4,128)S(1)} %broadcast_maximum_fusion, pred[512,4096]{0,1:T(8,128)(4,1)S(1)} %fusion.13), kind=kLoop, calls=%fused_computation.6 | loop fusion | flops 33552384 | bytes 35667968 | tf_op jit(solution)/shard_map/reduce_sum | solution.py:146
  571.4 15.4 %divide_convert_fusion = bf16[4,512,128]{1,2,0:T(8,128)(2,1)} fusion(bf16[4096,256]{1,0:T(8,128)(2,1)} %all-gather.8.cloned.1.call-done, f32[4096,512,4]{1,0,2:T(8,128)} %get-tuple-element.16, f32[4,512]{1,0:T(4,128)S(1)} %broadcast_maximum_fusion, pred[512,4096]{0,1:T(8,128)(4,1)S(1)} %fusion.13, f32[4,512]{1,0:T(4,128)S(1)} %fusion.4), kind=kOutput, calls=%fused_computation.51 | convolution fusion | flops 2181562368 | bytes 37240832 | tf_op jit(solution)/shard_map/giqk,kgd->giqd/dot_general | solution.py:147
  586.8 2.0 copy.36
  (56 shorter events, 9.8 us)
Async XLA Ops:
  7.4 3.4 copy-start
  7.4 174.4 %all-reduce.2.cloned.1.call-start = ((), (), s32[]{:S(2)}) async-start(), calls=%async_computation.3 | async-start | bytes 5242880 | tf_op jit(solution)/shard_map/psum | solution.py:73
  13.0 0.8 copy-start.7
  16.9 2.2 copy-start.6
  19.1 162.7 %copy-start.2 = (bf16[1,512,1280]{2,1,0:T(8,128)(2,1)S(1)}, bf16[1,512,1280]{2,1,0:T(8,128)(2,1)}, u32[]{:S(2)}) copy-start(bf16[1,512,1280]{2,1,0:T(8,128)(2,1)} %param.14) | copy-start | bytes 3932164
  21.1 163.0 %copy-start.9 = (f32[1280]{0:T(1024)S(1)}, f32[1280]{0:T(1024)}, u32[]{:S(2)}) copy-start(f32[1280]{0:T(1024)} %param.19) | copy-start | bytes 15364
  21.1 167.2 %all-gather.4.cloned.1.call-start = ((), (), s32[]{:S(2)}) async-start(), calls=%async_computation.4 | async-start | bytes 11141120 | tf_op jit(solution)/shard_map/all_gather | solution.py:84
  21.7 269.0 %reduce-scatter.2.cloned.1.call-start = ((), (), s32[]{:S(2)}) async-start(), calls=%async_computation.5 | async-start | bytes 4718592 | tf_op jit(solution)/shard_map/reduce_scatter | solution.py:87
  181.8 2.5 copy-start.3
  199.8 0.7 copy-start.10
  199.8 108.8 %copy-start.5 = (bf16[1,512,1024]{2,1,0:T(8,128)(2,1)S(1)}, bf16[1,512,1024]{2,1,0:T(8,128)(2,1)}, u32[]{:S(2)}) copy-start(bf16[1,512,1024]{2,1,0:T(8,128)(2,1)} %param.22) | copy-start | bytes 3145732
  201.8 91.2 %all-to-all-start = ((s32[8,32,1]{1,2,0:T(1,128)}), s32[8,32,1]{1,2,0:T(1,128)S(1)}, u32[]{:S(2)}, u32[]{:S(2)}) async-start(s32[8,32,1]{1,2,0:T(1,128)} %bitcast.3), calls=%async_computation | async-start | bytes 8192 | tf_op jit(solution)/shard_map/all_to_all | solution.py:108
  292.9 15.6 %all-to-all-start.1 = ((bf16[8,32,1024]{2,1,0:T(8,128)(2,1)}), bf16[8,32,1024]{2,1,0:T(8,128)(2,1)S(1)}, u32[]{:S(2)}, u32[]{:S(2)}) async-start(bf16[8,32,1024]{2,1,0:T(8,128)(2,1)} %bitcast.15), calls=%async_computation.2 | async-start | bytes 1048576 | tf_op jit(solution)/shard_map/all_to_all | solution.py:107
  299.8 177.6 %all-gather.6.cloned.1.call-start = ((), (), s32[]{:S(2)}) async-start(), calls=%async_computation.6 | async-start | bytes 9437184 | tf_op jit(solution)/shard_map/all_gather | solution.py:117
  310.1 172.5 %copy-start.11 = (f32[8192]{0:T(1024)S(1)}, f32[8192]{0:T(1024)}, u32[]{:S(2)}) copy-start(f32[8192]{0:T(1024)} %param.25) | copy-start | bytes 98308
  310.1 231.9 %all-gather.8.cloned.1.call-start = ((), (), s32[]{:S(2)}) async-start(), calls=%async_computation.7 | async-start | bytes 2359296 | tf_op jit(solution)/shard_map/all_gather | solution.py:131
  477.4 5.8 copy-start.4
  483.1 5.5 copy-start.8
  571.4 17.5 %copy-start.1 = (bf16[1280,3,160]{0,2,1:T(8,128)(2,1)S(1)}, bf16[1280,3,160]{0,2,1:T(8,128)(2,1)}, u32[]{:S(2)}) copy-start(bf16[1280,3,160]{0,2,1:T(8,128)(2,1)} %param.17) | copy-start | bytes 3686404
Sparse Core Ops, SparseCore 0:
  21.2 160.4 all-reduce.1
  200.0 90.6 reduce-scatter.1
  310.3 167.0 all-gather.5
Sparse Core Ops, SparseCore 1:
  23.9 94.0 all-gather.3
  488.7 53.3 all-gather.7
where the time goes:
time: 600 us; the launch traced here: 596 us
  waiting for transfers between devices  459 us (76%)
  matrix products  70.9 us (12%)
  other arithmetic  30 us (5%)
  between operations  14.7 us (2%)
  starting transfers between devices  14 us (2%)
  local copies, waits for them, and re-layouts  7.42 us (1%)
    all_gather x1, waiting for transfers between devices, shards(): full_rows = lax.all_gather(mixed, 'tp', axis=1, tiled=True)  167 us
    psum x1, waiting for transfers between devices, shards(): residual = own_patches.astype(jnp.float32) + lax.psum(partial_out, 'tp')  160 us
    reduce_scatter x1, waiting for transfers between devices, shards(): lax.psum_scatter(terms, 'tp', scatter_dimension=1, tiled=True)  82.1 us
    all_gather x1, waiting for transfers between devices, shards(): shard_block = lax.all_gather(keyvals, 'ctx', axis=0, tiled=True)  40.7 us
    dot_general x1, matrix products, shards(): jnp.einsum('giqk,kgd->giqd', weights.astype(jnp.bfloat16), block_values,...  15.4 us
    dot_general x1, matrix products, shards(): jnp.einsum('qgid,kgd->giqk', llm_queries, block_keys, preferred_element_t...  14.9 us
    reduce_sum x1, other arithmetic, shards(): new_sum = jnp.sum(weights, axis=-1)  14.5 us
  transfers between devices with their start and end apart: 7, of which 5 were waited for; matrix products, arithmetic and copies ran while one was open for 4% of the time, Pallas kernels for 0%

commit v1 on v0

v1 whole, which is shorter than its diff:
```python
import jax
import jax.numpy as jnp
from jax import lax
from jax.experimental import pallas as pl
from jax.experimental.pallas import tpu as pltpu
from jax.sharding import PartitionSpec as P

VHD = 80
HD = 128
EPS = 1e-06
MASKED = -1e30
BF = jnp.bfloat16
F32 = jnp.float32
MESH = pl.DeviceIdType.MESH
NT = (((1,), (1,)), ((), ()))


def dot(a, b):
    return jnp.dot(a, b, preferred_element_type=F32)


def dot_nt(a, b):
    return lax.dot_general(a, b, NT, preferred_element_type=F32)


def encode_kernel(
    patches, window_row, vit_gain, qkv_t, vit_out, merge_gain, merge_up, merge_down,
    text, place_row, llm_gain, w_query, w_keyval,
    q_text, kv_text, q_slots, kv_vis, pos_all,
    text_all, up_v, wd_all, wq_v, wkv_v, normed, q_v, k_v, v_v, heads_v,
    rs_send, rs_recv, own_part, merge_f, merged, acc_up, inner,
    rs2_send, rs2_recv, own_part2, vis_all, acc_t, ss_t, acc_v, ss_v, slots_out, kv_own,
    loc, txt_s, txt_r, wd_s, wd_r, sib_s, sib_r, rs_s, rs_r, mg_s, mg_r, r2_s, r2_r,
    vs_s, vs_r, kt_s, kt_r, qs_s, qs_r, kv_s, kv_r, ps_s, ps_r,
):
    c = lax.axis_index("ctx")
    t = lax.axis_index("tp")
    d = lax.axis_index("dp")
    y = t // 2
    x = lax.rem(t, 2)

    def tp_at(i):
        return (c, lax.rem(t + i, 8), d)

    def ctx_at(i):
        return (lax.rem(c + i, 8), t, d)

    def grid_at(dy, dx):
        return (c, lax.rem(y + dy, 4) * 2 + lax.rem(x + dx, 2), d)

    sibling = (c, t, 1 - d)

    def remote(src, dst, ssem, rsem, dev):
        cp = pltpu.make_async_remote_copy(
            src_ref=src, dst_ref=dst, send_sem=ssem, recv_sem=rsem, device_id=dev, device_id_type=MESH
        )
        cp.start()
        return cp

    barrier = pltpu.get_barrier_semaphore()
    for i in range(1, 8):
        pl.semaphore_signal(barrier, inc=1, device_id=tp_at(i), device_id_type=MESH)
        pl.semaphore_signal(barrier, inc=1, device_id=ctx_at(i), device_id_type=MESH)
    pl.semaphore_signal(barrier, inc=1, device_id=sibling, device_id_type=MESH)

    own_wd = c * 2 + d
    loads = [
        pltpu.make_async_copy(merge_down, wd_all.at[own_wd], loc.at[0]),
        pltpu.make_async_copy(merge_up, up_v, loc.at[1]),
        pltpu.make_async_copy(text, text_all.at[0], loc.at[2]),
        pltpu.make_async_copy(w_query, wq_v, loc.at[3]),
        pltpu.make_async_copy(w_keyval, wkv_v, loc.at[4]),
    ]
    for cp in loads:
        cp.start()
    pl.semaphore_wait(barrier, 15)

    pos_copies = []
    pos_all[pl.ds(c, 1), :] = place_row[...]
    for i in range(1, 8):
        pos_copies.append(
            remote(place_row, pos_all.at[pl.ds(c, 1)], ps_s.at[i], ps_r.at[i], ctx_at(i))
        )

    slot_of = lambda dy, dx: text_all.at[dy * 2 + dx]
    half = text.shape[0] // 2
    lo, hi = pl.ds(0, half), pl.ds(half, half)
    txt = {}

    def text_send(name, src, dst, dev):
        n = len(txt)
        txt[name] = remote(src, dst, txt_s.at[n], txt_r.at[n], dev)

    text_send("x0", text, slot_of(0, 1), grid_at(0, 1))
    text_send("yp", text, slot_of(3, 0), grid_at(1, 0))
    text_send("ym", text, slot_of(1, 0), grid_at(3, 0))

    wd_copies = [None]
    for i in range(1, 8):
        wd_copies.append(
            remote(merge_down, wd_all.at[own_wd], wd_s.at[i], wd_r.at[i], ctx_at(i))
        )
    sib_copies = [remote(merge_down, wd_all.at[own_wd], sib_s.at[0], sib_r.at[0], sibling)]

    rows = patches.shape[0]
    step = 128

    @pl.loop(0, rows // step)
    def _(r):
        sl = pl.ds(pl.multiple_of(r * step, step), step)
        v = patches[sl, :].astype(F32)
        ms = jnp.mean(v * v, axis=-1, keepdims=True)
        n = (v * lax.rsqrt(ms + EPS) * vit_gain[...]).astype(BF)
        q_v[sl, :] = dot_nt(n, qkv_t[0:160, :]).astype(BF)
        k_v[sl, :] = dot_nt(n, qkv_t[160:320, :]).astype(BF)
        v_v[sl, :] = dot_nt(n, qkv_t[320:480, :]).astype(BF)

    @pl.loop(0, rows // step)
    def _(r):
        sl = pl.ds(pl.multiple_of(r * step, step), step)
        qb = q_v[sl, :]
        col = lax.broadcasted_iota(jnp.int32, (step, 160), 1)
        ids = jnp.transpose(jnp.broadcast_to(window_row[:, sl], (8, step)))[:, 0:1]
        same = ids == window_row[...]
        outs = []
        for h in range(2):
            mine = (col < VHD) if h == 0 else (col >= VHD)
            qh = jnp.where(mine, qb, jnp.zeros_like(qb))
            s = dot_nt(qh, k_v[...]) * VHD ** (-0.5)
            s = jnp.where(same, s, MASKED)
            w = jnp.where(same, jnp.exp(s - jnp.max(s, axis=-1, keepdims=True)), 0.0)
            tot = jnp.sum(w, axis=-1, keepdims=True)
            outs.append(dot(w.astype(BF), v_v[...]) / tot)
        heads_v[sl, :] = jnp.where(col < VHD, outs[0], outs[1]).astype(BF)

    rs_copies = [None]
    for i in list(range(1, 8)) + [0]:
        dst = lax.rem(t + i, 8)
        hb = heads_v[pl.ds(pl.multiple_of(dst * 64, 64), 64), :]
        part = dot(hb, vit_out[...])
        if i == 0:
            own_part[...] = part
        else:
            rs_send[i] = part.astype(BF)
            rs_copies.append(remote(rs_send.at[i], rs_recv.at[i], rs_s.at[i], rs_r.at[i], tp_at(i)))

    txt["x0"].wait_recv()
    text_send("xyp", slot_of(0, 1), slot_of(3, 1), grid_at(1, 0))
    text_send("xym", slot_of(0, 1), slot_of(1, 1), grid_at(3, 0))
    txt["yp"].wait_recv()
    text_send("f1", slot_of(3, 0).at[lo], slot_of(2, 0).at[lo], grid_at(1, 0))
    txt["ym"].wait_recv()
    text_send("f2", slot_of(1, 0).at[hi], slot_of(2, 0).at[hi], grid_at(3, 0))

    for cp in rs_copies[1:]:
        cp.wait_recv()
    own_rows = pl.ds(pl.multiple_of(t * 64, 64), 64)
    res = patches[own_rows, :].astype(F32) + own_part[...]
    for i in range(1, 8):
        res += rs_recv[i].astype(F32)
    ms = jnp.mean(res * res, axis=-1, keepdims=True)
    res = res * lax.rsqrt(ms + EPS) * merge_gain[...]
    for b in range(10):
        merge_f[b] = res[:, b * 128 : (b + 1) * 128]
    own_m = pl.ds(pl.multiple_of(t * 16, 16), 16)
    for j in range(4):
        for b in range(10):
            at = j * 1280 + b * 128
            merged[own_m, at : at + 128] = merge_f[b, pl.ds(j, 16, stride=4), :].astype(BF)
    mg_copies = []
    for i in range(1, 8):
        mg_copies.append(
            remote(merged.at[own_m], merged.at[own_m], mg_s.at[i], mg_r.at[i], tp_at(i))
        )

    for i in range(1, 8):
        wd_copies[i].wait_recv()
        src = wd_all.at[lax.rem(c + 8 - i, 8) * 2 + d]
        sib_copies.append(remote(src, src, sib_s.at[i], sib_r.at[i], sibling))

    txt["f1"].wait_recv()
    text_send("g1", slot_of(2, 0).at[lo], slot_of(2, 1).at[lo], grid_at(0, 1))
    txt["f2"].wait_recv()
    text_send("g2", slot_of(2, 0).at[hi], slot_of(2, 1).at[hi], grid_at(0, 1))

    for cp in mg_copies:
        cp.wait_recv()
    loads[1].wait()
    acc_up[...] = jnp.zeros_like(acc_up)

    @pl.loop(0, 4)
    def _(k):
        sl = pl.ds(pl.multiple_of(k * 1280, 1280), 1280)
        acc_up[...] += dot(merged[:, sl], up_v[sl, :])

    pre = acc_up[...]
    inner[...] = (0.5 * pre * (1.0 + lax.erf(pre * (0.5**0.5)))).astype(BF)

    loads[0].wait()
    for cp in sib_copies:
        cp.wait_recv()
    r2_copies = [None]
    for i in list(range(1, 8)) + [0]:
        dst = lax.rem(t + i, 8)
        for e in range(2):
            part = dot(inner[...], wd_all[dst * 2 + e])
            if i == 0:
                own_part2[:, e * 512 : (e + 1) * 512] = part
            else:
                rs2_send[i, :, e * 512 : (e + 1) * 512] = part.astype(BF)
        if i:
            r2_copies.append(
                remote(rs2_send.at[i], rs2_recv.at[i], r2_s.at[i], r2_r.at[i], tp_at(i))
            )
    for cp in r2_copies[1:]:
        cp.wait_recv()
    total = own_part2[...]
    for i in range(1, 8):
        total += rs2_recv[i].astype(F32)
    vis_all[0] = total.astype(BF)
    vs_copies = [None]
    for i in range(1, 8):
        vs_copies.append(remote(vis_all.at[0], vis_all.at[i], vs_s.at[i], vs_r.at[i], tp_at(i)))

    loads[2].wait()
    loads[3].wait()
    loads[4].wait()
    for n in ("xyp", "xym", "g1", "g2"):
        txt[n].wait_recv()

    def project(source, slot, block, acc, ss, row_count, chunk):
        feats = pl.ds(pl.multiple_of(block * 1024, 1024), 1024)
        gain = llm_gain[pl.ds(block, 1), :]

        @pl.loop(0, row_count // chunk)
        def _(r):
            sl = pl.ds(pl.multiple_of(r * chunk, chunk), chunk)
            v = source[slot, sl, :].astype(F32)
            sq = v * v
            part = sq[:, 0:128]
            for j in range(1, 8):
                part += sq[:, j * 128 : (j + 1) * 128]
            ss[sl, :] += part
            xb = (v * gain).astype(BF)
            acc[sl, 0:512] += dot(xb, wq_v[feats, :])
            acc[sl, 512:768] += dot(xb, wkv_v[feats, :])

    def inverse(ss):
        return lax.rsqrt(jnp.sum(ss, axis=-1, keepdims=True) * (1.0 / 8192) + EPS)

    acc_t[...] = jnp.zeros_like(acc_t)
    ss_t[...] = jnp.zeros_like(ss_t)

    @pl.loop(0, 8)
    def _(slot):
        block = lax.rem(y + slot // 2, 4) * 2 + lax.rem(x + lax.rem(slot, 2), 2)
        project(text_all, slot, block, acc_t, ss_t, 512, 256)

    @pl.loop(0, 4)
    def _(r):
        sl = pl.ds(pl.multiple_of(r * 128, 128), 128)
        inv = inverse(ss_t[sl, :])
        q_text[sl, :] = (acc_t[sl, 0:512] * inv).astype(BF)
        kv_text[0, sl, :] = (acc_t[sl, 512:768] * inv).astype(BF)

    kt_copies = []
    for j in range(1, 5):
        kt_copies.append(remote(kv_text.at[0], kv_text.at[j], kt_s.at[j], kt_r.at[j], ctx_at(j)))

    for cp in vs_copies[1:]:
        cp.wait_recv()
    acc_v[...] = jnp.zeros_like(acc_v)
    ss_v[...] = jnp.zeros_like(ss_v)

    @pl.loop(0, 8)
    def _(slot):
        project(vis_all, slot, lax.rem(t + 8 - slot, 8), acc_v, ss_v, 128, 128)

    inv = inverse(ss_v[...])
    kv_own[...] = (acc_v[:, 512:768] * inv).astype(BF)
    kv_copies = []
    for i in range(1, 8):
        kv_copies.append(remote(kv_own, kv_vis.at[c], kv_s.at[i], kv_r.at[i], ctx_at(i)))
    kv_vis[c] = kv_own[...]
    qv = (acc_v[:, 0:512] * inv).astype(BF)
    dest = place_row[...] // 512
    hit = lax.broadcasted_iota(jnp.int32, (8, 128), 0) == dest
    hit_f = hit.astype(F32)
    before = (
        lax.broadcasted_iota(jnp.int32, (128, 128), 0) < lax.broadcasted_iota(jnp.int32, (128, 128), 1)
    ).astype(F32).astype(BF)
    rank = jnp.sum(dot(hit_f.astype(BF), before) * hit_f, axis=0, keepdims=True)
    slot_row = dest * 32 + rank.astype(jnp.int32)
    pick = (lax.broadcasted_iota(jnp.int32, (256, 128), 0) == slot_row).astype(F32).astype(BF)
    slots_out[...] = dot(pick, qv).astype(BF)
    qs_copies = []
    for i in range(1, 8):
        sl = pl.ds(pl.multiple_of(lax.rem(c + i, 8) * 32, 32), 32)
        qs_copies.append(remote(slots_out.at[sl], q_slots.at[c], qs_s.at[i], qs_r.at[i], ctx_at(i)))
    q_slots[c] = slots_out[pl.ds(pl.multiple_of(c * 32, 32), 32), :]

    for cp in kt_copies + kv_copies + qs_copies + pos_copies:
        cp.wait_recv()
    for cp in (
        list(txt.values()) + wd_copies[1:] + sib_copies + rs_copies[1:] + mg_copies + r2_copies[1:]
        + vs_copies[1:] + kt_copies + kv_copies + qs_copies + pos_copies
    ):
        cp.wait_send()


def attend_kernel(
    q_text, kv_text, q_slots, kv_vis, pos_all, segments, out,
    place, expand, q_v, k_v, v_v, bias, m_v, l_v, acc,
):
    c = lax.axis_index("ctx")
    lanes = kv_vis.shape[1]
    own = pl.ds(pl.multiple_of(c * 512, 512), 512)
    pos = pos_all[...]
    hit = (pos // 512) == c
    hit_f = hit.astype(F32)
    before = (
        lax.broadcasted_iota(jnp.int32, (128, 128), 0) < lax.broadcasted_iota(jnp.int32, (128, 128), 1)
    ).astype(F32).astype(BF)
    rank = dot(hit_f.astype(BF), before).astype(jnp.int32)
    slot = jnp.where(hit, rank, -1)
    ones = jnp.ones((1024, 128), BF)

    def fill_place(base):
        for s in range(8):
            rows = lax.broadcasted_iota(jnp.int32, (512, lanes), 0) + base
            place[:, s * lanes : (s + 1) * lanes] = (rows == pos[s : s + 1, :]).astype(F32).astype(BF)

    for s in range(8):
        back = (lax.broadcasted_iota(jnp.int32, (32, lanes), 0) == slot[s : s + 1, :]).astype(F32)
        expand[s * lanes : (s + 1) * lanes, :] = dot(
            jnp.transpose(back).astype(BF), q_slots[s]
        ).astype(BF)
    seg_q = jnp.transpose(jnp.broadcast_to(segments[:, own], (8, 512)))[:, 0:1]

    for j in range(5):
        base = (c - j) * 512

        @pl.when(base >= 0)
        def _():
            fill_place(base)
            is_vis = dot(place[...], ones) > 0.5
            k_v[...] = jnp.where(
                is_vis, dot(place[...], kv_vis[:, :, 0:128].reshape(1024, 128)),
                kv_text[j, :, 0:128].astype(F32),
            ).astype(BF)
            v_v[...] = jnp.where(
                is_vis, dot(place[...], kv_vis[:, :, 128:256].reshape(1024, 128)),
                kv_text[j, :, 128:256].astype(F32),
            ).astype(BF)
            if j == 0:
                for h in range(4):
                    sl = slice(h * 128, (h + 1) * 128)
                    q_v[:, sl] = jnp.where(
                        is_vis, dot(place[...], expand[:, sl]), q_text[:, sl].astype(F32)
                    ).astype(BF)
            seg_k = segments[:, pl.ds(pl.multiple_of(base, 512), 512)]
            allowed = seg_q == seg_k
            if j == 0:
                allowed = allowed & (
                    lax.broadcasted_iota(jnp.int32, (512, 512), 1)
                    <= lax.broadcasted_iota(jnp.int32, (512, 512), 0)
                )
            bias[...] = jnp.where(allowed, 0.0, MASKED)

            @pl.loop(0, 16)
            def _(it):
                h = it // 4
                r = lax.rem(it, 4)
                sl = pl.ds(pl.multiple_of(r * 128, 128), 128)
                hl = pl.ds(pl.multiple_of(h * 128, 128), 128)
                s_ = dot_nt(q_v[sl, hl], k_v[...]) * HD ** (-0.5) + bias[sl, :]
                top = jnp.max(s_, axis=-1, keepdims=True)
                if j == 0:
                    w = jnp.exp(s_ - top)
                    m_v[h, sl, :] = jnp.broadcast_to(top, (128, 128))
                    l_v[h, sl, :] = jnp.broadcast_to(jnp.sum(w, axis=-1, keepdims=True), (128, 128))
                    acc[h, sl, :] = dot(w.astype(BF), v_v[...])
                else:
                    old = m_v[h, sl, :]
                    new = jnp.maximum(old, top)
                    alpha = jnp.exp(old - new)
                    w = jnp.exp(s_ - new[:, 0:1])
                    m_v[h, sl, :] = new
                    l_v[h, sl, :] = l_v[h, sl, :] * alpha + jnp.sum(w, axis=-1, keepdims=True)
                    acc[h, sl, :] = acc[h, sl, :] * alpha + dot(w.astype(BF), v_v[...])

    for h in range(4):
        out[:, h * 128 : (h + 1) * 128] = (acc[h] / l_v[h]).astype(BF)


def shards(
    patches, window_ids, vit_gain, vit_qkv, vit_out, merge_gain, merge_up, merge_down,
    text_rows, placeholders, segments, llm_gain, w_query, w_keyval,
):
    vm = pl.BlockSpec(memory_space=pltpu.VMEM)
    hbm = pl.BlockSpec(memory_space=pl.ANY)
    dma = pltpu.SemaphoreType.DMA
    sds = jax.ShapeDtypeStruct
    qkv_t = vit_qkv.transpose(1, 2, 0).reshape(480, 1280)
    encoded = pl.pallas_call(
        encode_kernel,
        out_shape=(
            sds((512, 512), BF), sds((5, 512, 256), BF), sds((8, 32, 512), BF),
            sds((8, 128, 256), BF), sds((8, 128), jnp.int32),
        ),
        in_specs=[vm, vm, vm, vm, vm, vm, hbm, hbm, hbm, vm, vm, hbm, hbm],
        out_specs=(vm, vm, vm, vm, vm),
        scratch_shapes=[
            pltpu.VMEM((8, 512, 1024), BF),
            pltpu.VMEM((5120, 640), BF),
            pltpu.VMEM((16, 640, 512), BF),
            pltpu.VMEM((8192, 512), BF),
            pltpu.VMEM((8192, 256), BF),
            pltpu.VMEM((8, 128), BF),
            pltpu.VMEM((512, 160), BF),
            pltpu.VMEM((512, 160), BF),
            pltpu.VMEM((512, 160), BF),
            pltpu.VMEM((512, 160), BF),
            pltpu.VMEM((8, 64, 1280), BF),
            pltpu.VMEM((8, 64, 1280), BF),
            pltpu.VMEM((64, 1280), F32),
            pltpu.VMEM((10, 64, 128), F32),
            pltpu.VMEM((128, 5120), BF),
            pltpu.VMEM((128, 640), F32),
            pltpu.VMEM((128, 640), BF),
            pltpu.VMEM((8, 128, 1024), BF),
            pltpu.VMEM((8, 128, 1024), BF),
            pltpu.VMEM((128, 1024), F32),
            pltpu.VMEM((8, 128, 1024), BF),
            pltpu.VMEM((512, 768), F32),
            pltpu.VMEM((512, 128), F32),
            pltpu.VMEM((128, 768), F32),
            pltpu.VMEM((128, 128), F32),
            pltpu.VMEM((256, 512), BF),
            pltpu.VMEM((128, 256), BF),
            dma((5,)), dma((9,)), dma((9,)),
        ] + [dma((8,))] * 20,
        compiler_params=pltpu.CompilerParams(
            collective_id=0, has_side_effects=True, vmem_limit_bytes=63 * 2**20
        ),
    )(
        patches[0], window_ids, vit_gain.reshape(1, 1280), qkv_t, vit_out,
        merge_gain.reshape(1, 1280), merge_up, merge_down, text_rows[0], placeholders,
        llm_gain.reshape(8, 1024), w_query, w_keyval.reshape(8192, 256),
    )
    out = pl.pallas_call(
        attend_kernel,
        out_shape=sds((512, 512), BF),
        in_specs=[vm] * 6,
        out_specs=vm,
        scratch_shapes=[
            pltpu.VMEM((512, 1024), BF),
            pltpu.VMEM((1024, 512), BF),
            pltpu.VMEM((512, 512), BF),
            pltpu.VMEM((512, 128), BF),
            pltpu.VMEM((512, 128), BF),
            pltpu.VMEM((512, 512), F32),
            pltpu.VMEM((4, 512, 128), F32),
            pltpu.VMEM((4, 512, 128), F32),
            pltpu.VMEM((4, 512, 128), F32),
        ],
        compiler_params=pltpu.CompilerParams(vmem_limit_bytes=40 * 2**20),
    )(*encoded, segments)
    return out[None]


def solution(mesh):
    in_specs = (
        P("dp", "ctx", None),
        P("dp", "ctx"),
        P(),
        P(None, None, "tp"),
        P("tp", None),
        P(),
        P(None, "tp"),
        P("tp", ("ctx", "dp")),
        P("dp", "ctx", "tp"),
        P("dp", "ctx"),
        P("dp", None),
        P(),
        P(None, "tp"),
        P(None, None, "tp"),
    )
    out_specs = P("dp", "ctx", "tp")
    return jax.shard_map(shards, mesh=mesh, in_specs=in_specs, out_specs=out_specs, check_vma=False)
```

time: 600 us -> 308 us (0.51)
  the two profiles are of different devices: /device:TPU:96 before, /device:TPU:6 now
where the time goes in v1:
time: 308 us; the launch traced here: 307 us
  Pallas kernels  293 us (95%)
  local copies, waits for them, and re-layouts  13.6 us (4%)
    pallas_call x1, Pallas kernels, shards(): pl.pallas_call(encode_kernel, out_shape=(sds((512, 512), BF), sds((5, 512...  247 us
    pallas_call x1, Pallas kernels, shards(): pl.pallas_call(attend_kernel, out_shape=sds((512, 512), BF), in_specs=[vm...  46.1 us
    unnamed x13, local copies, waits for them, and re-layouts  9.69 us

profile of v1, /device:TPU:6, one launch (start us, length us, event | category | flops | bytes accessed | tf_op | source)
XLA Modules:
  0.0 307.2 jit_solution(16990901375254664350)
XLA Ops:
  0.0 1.3 reshape.15.vit_gain
  1.3 1.3 reshape.17.merge_gain
  2.6 1.4 reshape.18.llm_gain
  4.0 4.7 %copy.17 = bf16[1024,8,2,128]{3,1,2,0:T(8,128)(2,1)} copy(bf16[1024,8,2,128]{3,2,1,0:T(2,128)(2,1)} %bitcast.11) | data formatting | bytes 8388608
  8.6 0.0 copy-start.4
  8.6 247.3 %shard_map.136 = (bf16[512,512]{1,0:T(8,128)(2,1)}, bf16[5,512,256]{2,1,0:T(8,128)(2,1)}, bf16[8,32,512]{2,1,0:T(8,128)(2,1)}, bf16[8,128,256]{2,1,0:T(8,128)(2,1)}, s32[8,128]{1,0:T(8,128)}) custom-call(bf16[512,1280]{1,0:T(8,128)(2,1)} %bitcast.12, s32[1,512]{1,0:T(1,128)} %window_row.1, f32[1,1280]{1,0:T(1,128)} %reshape.15.vit_gain, ...), custom_call_target="tpu_custom_call" | custom-call | tf_op jit(solution)/shard_map/pallas_call | solution.py:405
  256.0 0.0 copy-done.4
  256.0 0.0 copy-start
  256.0 1.3 copy-done
  257.3 0.0 copy-start.1
  257.3 1.0 copy-done.1
  258.4 0.0 copy-start.2
  258.4 1.0 copy-done.2
  259.4 0.0 copy-start.3
  259.4 0.9 copy-done.3
  260.3 0.0 copy-start.5
  260.4 0.7 copy-done.5
  261.0 46.1 %shard_map.137 = bf16[512,512]{1,0:T(8,128)(2,1)} custom-call(bf16[512,512]{1,0:T(8,128)(2,1)S(1)} %copy-done.1, bf16[5,512,256]{2,1,0:T(8,128)(2,1)S(1)} %copy-done, bf16[8,32,512]{2,1,0:T(8,128)(2,1)S(1)} %copy-done.3, bf16[8,128,256]{2,1,0:T(8,128)(2,1)S(1)} %copy-done.2, s32[8,128]{1,0:T(8,128)S(1)} %copy-done.5, s32[1,4096]{1,0:T(1,128)S(1)} %copy-done.4), custom_call_target="tpu_custom_call" | custom-call | tf_op jit(solution)/shard_map/pallas_call | solution.py:451
Async XLA Ops:
  8.6 247.4 %copy-start.4 = (s32[1,4096]{1,0:T(1,128)S(1)}, s32[1,4096]{1,0:T(1,128)}, u32[]{:S(2)}) copy-start(s32[1,4096]{1,0:T(1,128)} %segments.1) | copy-start | bytes 49156
  256.0 1.3 copy-start
  257.3 1.0 copy-start.1
  258.4 1.0 copy-start.2
  259.4 0.9 copy-start.3
  260.3 0.7 copy-start.5

commit v2 on v1

v2 whole, which is shorter than its diff:
```python
import jax
import jax.numpy as jnp
from jax import lax
from jax.experimental import pallas as pl
from jax.experimental.pallas import tpu as pltpu
from jax.sharding import PartitionSpec as P

VHD = 80
HD = 128
EPS = 1e-06
MASKED = -1e30
BF = jnp.bfloat16
F32 = jnp.float32
MESH = pl.DeviceIdType.MESH
NT = (((1,), (1,)), ((), ()))


def dot(a, b):
    return jnp.dot(a, b, preferred_element_type=F32)


def dot_nt(a, b):
    return lax.dot_general(a, b, NT, preferred_element_type=F32)


class Sent:
    def __init__(self, copy):
        self.copy = copy
        self.arrived = False

    def wait_recv(self):
        if not self.arrived:
            self.arrived = True
            self.copy.wait_recv()


def encode_kernel(
    patches, window_row, vit_gain, qkv_t, vit_out, merge_gain, merge_up, merge_down,
    text, place_row, llm_gain, w_query, w_keyval,
    q_text, kv_text, q_slots, kv_vis, pos_all,
    text_all, up_v, wd_all, wq_v, wkv_raw, wkv_f, wkv_v, q_v, k_v, v_v, heads_v,
    rs_send, rs_recv, own_part, merge_f, merged, acc_up, inner,
    rs2_send, rs2_recv, own_part2, vis_all, acc_t, ss_t, acc_v, ss_v, slots_out, kv_own,
    loc, txt_s, txt_r, sib_s, sib_r, rs_s, rs_r, mg_s, mg_r, wd_s, wd_r, r2_s, r2_r,
    vs_s, vs_r, kt_s, kt_r, qs_s, qs_r, kv_s, kv_r, ps_s, ps_r,
):
    c = lax.axis_index("ctx")
    t = lax.axis_index("tp")
    d = lax.axis_index("dp")
    y = t // 2
    x = lax.rem(t, 2)
    started = []

    def tp_at(i):
        return (c, lax.rem(t + i, 8), d)

    def ctx_at(i):
        return (lax.rem(c + i, 8), t, d)

    def grid_at(dy, dx):
        return (c, lax.rem(y + dy, 4) * 2 + lax.rem(x + dx, 2), d)

    sibling = (c, t, 1 - d)

    def remote(src, dst, ssem, rsem, dev):
        cp = pltpu.make_async_remote_copy(
            src_ref=src, dst_ref=dst, send_sem=ssem, recv_sem=rsem, device_id=dev, device_id_type=MESH
        )
        cp.start()
        started.append(Sent(cp))
        return started[-1]

    def finish():
        for cp in started:
            cp.wait_recv()
        for cp in started:
            cp.copy.wait_send()
        for cp in loads:
            cp.wait_recv()

    barrier = pltpu.get_barrier_semaphore()
    for i in range(1, 8):
        pl.semaphore_signal(barrier, inc=1, device_id=tp_at(i), device_id_type=MESH)
        pl.semaphore_signal(barrier, inc=1, device_id=ctx_at(i), device_id_type=MESH)
    pl.semaphore_signal(barrier, inc=1, device_id=sibling, device_id_type=MESH)
    loads = [
        Sent(pltpu.make_async_copy(merge_down, wd_all.at[c * 2 + d], loc.at[0])),
        Sent(pltpu.make_async_copy(merge_up, up_v, loc.at[1])),
        Sent(pltpu.make_async_copy(text, text_all.at[0], loc.at[2])),
        Sent(pltpu.make_async_copy(w_query, wq_v, loc.at[3])),
    ] + [
        Sent(pltpu.make_async_copy(w_keyval.at[pl.ds(k * 2048, 2048)], wkv_raw.at[k % 2], loc.at[4 + k % 2]))
        for k in range(8)
    ]
    for cp in loads[:6]:
        cp.copy.start()
    pl.semaphore_wait(barrier, 15)

    pos_copies = []
    pos_all[pl.ds(c, 1), :] = place_row[...]
    for i in range(1, 8):
        pos_copies.append(
            remote(place_row, pos_all.at[pl.ds(c, 1)], ps_s.at[i], ps_r.at[i], ctx_at(i))
        )

    slot_of = lambda dy, dx: text_all.at[dy * 2 + dx]
    half = text.shape[0] // 2
    lo, hi = pl.ds(0, half), pl.ds(half, half)
    txt = {}

    def text_send(name, src, dst, dev):
        n = len(txt)
        txt[name] = remote(src, dst, txt_s.at[n], txt_r.at[n], dev)

    text_send("x0", text, slot_of(0, 1), grid_at(0, 1))
    text_send("yp", text, slot_of(3, 0), grid_at(1, 0))
    text_send("ym", text, slot_of(1, 0), grid_at(3, 0))

    x_hi = c // 4
    z = lax.rem(c, 4)

    def z_at(i):
        return (x_hi * 4 + lax.rem(z + i, 4), t, d)

    def wd_block(ctx):
        return wd_all.at[ctx * 2 + d]

    partner = lax.rem(c + 4, 8)
    wd_copies = [remote(merge_down, wd_block(c), wd_s.at[0], wd_r.at[0], (partner, t, d))]
    for i in (1, 3, 2):
        wd_copies.append(remote(merge_down, wd_block(c), wd_s.at[i], wd_r.at[i], z_at(i)))
    sib_copies = [remote(merge_down, wd_block(c), sib_s.at[0], sib_r.at[0], sibling)]

    def to_sibling(n, ctx):
        sib_copies.append(remote(wd_block(ctx), wd_block(ctx), sib_s.at[n], sib_r.at[n], sibling))

    rows = patches.shape[0]
    step = 128

    @pl.loop(0, rows // step)
    def _(r):
        sl = pl.ds(pl.multiple_of(r * step, step), step)
        v = patches[sl, :].astype(F32)
        ms = jnp.mean(v * v, axis=-1, keepdims=True)
        n = (v * lax.rsqrt(ms + EPS) * vit_gain[...][None, :]).astype(BF)
        q_v[sl, :] = dot_nt(n, qkv_t[0:160, :]).astype(BF)
        k_v[sl, :] = dot_nt(n, qkv_t[160:320, :]).astype(BF)
        v_v[sl, :] = dot_nt(n, qkv_t[320:480, :]).astype(BF)

    @pl.loop(0, rows // step)
    def _(r):
        sl = pl.ds(pl.multiple_of(r * step, step), step)
        qb = q_v[sl, :]
        col = lax.broadcasted_iota(jnp.int32, (step, 160), 1)
        ids = jnp.transpose(jnp.broadcast_to(window_row[:, sl], (8, step)))[:, 0:1]
        same = ids == window_row[...]
        outs = []
        for h in range(2):
            mine = (col < VHD) if h == 0 else (col >= VHD)
            qh = jnp.where(mine, qb, jnp.zeros_like(qb))
            s = dot_nt(qh, k_v[...]) * VHD ** (-0.5)
            s = jnp.where(same, s, MASKED)
            w = jnp.where(same, jnp.exp(s - jnp.max(s, axis=-1, keepdims=True)), 0.0)
            tot = jnp.sum(w, axis=-1, keepdims=True)
            outs.append(dot(w.astype(BF), v_v[...]) / tot)
        heads_v[sl, :] = jnp.where(col < VHD, outs[0], outs[1]).astype(BF)

    rs_copies = [None]
    for i in list(range(1, 8)) + [0]:
        dst = lax.rem(t + i, 8)
        hb = heads_v[pl.ds(pl.multiple_of(dst * 64, 64), 64), :]
        part = dot(hb, vit_out[...])
        if i == 0:
            own_part[...] = part
        else:
            rs_send[i] = part.astype(BF)
            rs_copies.append(remote(rs_send.at[i], rs_recv.at[i], rs_s.at[i], rs_r.at[i], tp_at(i)))

    for k in range(8):
        loads[4 + k].wait_recv()
        wkv_f[...] = wkv_raw[k % 2].astype(F32)
        if k < 6:
            loads[6 + k].copy.start()
        sl = pl.ds(k * 1024, 1024)
        wkv_v[sl, 0:128] = wkv_f[pl.ds(0, 1024, stride=2), :].astype(BF)
        wkv_v[sl, 128:256] = wkv_f[pl.ds(1, 1024, stride=2), :].astype(BF)

    wd_copies[0].wait_recv()
    for n, i in enumerate((1, 3, 2)):
        wd_copies.append(remote(wd_block(partner), wd_block(partner), wd_s.at[4 + n], wd_r.at[4 + n], z_at(i)))
    to_sibling(1, partner)

    for cp in rs_copies[1:]:
        cp.wait_recv()
    own_rows = pl.ds(pl.multiple_of(t * 64, 64), 64)
    res = patches[own_rows, :].astype(F32) + own_part[...]
    for i in range(1, 8):
        res += rs_recv[i].astype(F32)
    ms = jnp.mean(res * res, axis=-1, keepdims=True)
    res = res * lax.rsqrt(ms + EPS) * merge_gain[...][None, :]
    for b in range(10):
        merge_f[b] = res[:, b * 128 : (b + 1) * 128]
    own_m = pl.ds(pl.multiple_of(t * 16, 16), 16)
    for j in range(4):
        for b in range(10):
            at = j * 1280 + b * 128
            merged[own_m, at : at + 128] = merge_f[b, pl.ds(j, 16, stride=4), :].astype(BF)
    mg_copies = []
    for i in range(1, 8):
        mg_copies.append(
            remote(merged.at[own_m], merged.at[own_m], mg_s.at[i], mg_r.at[i], tp_at(i))
        )

    loads[2].wait_recv()
    loads[3].wait_recv()
    def project(source, slot, block, acc, ss, row_count, chunk):
        feats = pl.ds(pl.multiple_of(block * 1024, 1024), 1024)
        gain = llm_gain[feats][None, :]

        @pl.loop(0, row_count // chunk)
        def _(r):
            sl = pl.ds(pl.multiple_of(r * chunk, chunk), chunk)
            v = source[slot, sl, :].astype(F32)
            sq = v * v
            part = sq[:, 0:128]
            for j in range(1, 8):
                part += sq[:, j * 128 : (j + 1) * 128]
            ss[sl, :] += part
            xb = (v * gain).astype(BF)
            acc[sl, 0:512] += dot(xb, wq_v[feats, :])
            acc[sl, 512:768] += dot(xb, wkv_v[feats, :])

    def inverse(ss):
        return lax.rsqrt(jnp.sum(ss, axis=-1, keepdims=True) * (1.0 / 8192) + EPS)

    def project_text(first, second):
        @pl.loop(0, 2)
        def _(n):
            slot = jnp.where(n == 0, first, second)
            block = lax.rem(y + slot // 2, 4) * 2 + lax.rem(x + lax.rem(slot, 2), 2)
            project(text_all, slot, block, acc_t, ss_t, 512, 256)

    acc_t[...] = jnp.zeros_like(acc_t)
    ss_t[...] = jnp.zeros_like(ss_t)
    txt["x0"].wait_recv()
    project_text(0, 1)

    for cp in mg_copies:
        cp.wait_recv()
    txt["yp"].wait_recv()
    text_send("f1", slot_of(3, 0).at[lo], slot_of(2, 0).at[lo], grid_at(1, 0))
    txt["ym"].wait_recv()
    text_send("f2", slot_of(1, 0).at[hi], slot_of(2, 0).at[hi], grid_at(3, 0))
    txt["x0"].wait_recv()
    text_send("xyp", slot_of(0, 1), slot_of(3, 1), grid_at(1, 0))
    text_send("xym", slot_of(0, 1), slot_of(1, 1), grid_at(3, 0))

    loads[1].wait_recv()
    acc_up[...] = jnp.zeros_like(acc_up)

    @pl.loop(0, 4)
    def _(k):
        sl = pl.ds(pl.multiple_of(k * 1280, 1280), 1280)
        acc_up[...] += dot(merged[:, sl], up_v[sl, :])

    pre = acc_up[...]
    inner[...] = (0.5 * pre * (1.0 + lax.erf(pre * (0.5**0.5)))).astype(BF)

    project_text(2, 6)
    txt["f1"].wait_recv()
    text_send("g1", slot_of(2, 0).at[lo], slot_of(2, 1).at[lo], grid_at(0, 1))
    txt["f2"].wait_recv()
    text_send("g2", slot_of(2, 0).at[hi], slot_of(2, 1).at[hi], grid_at(0, 1))
    for n, i in enumerate((1, 3, 2)):
        wd_copies[1 + n].wait_recv()
        to_sibling(2 + n, x_hi * 4 + lax.rem(z + 4 - i, 4))
    for n, i in enumerate((1, 3, 2)):
        wd_copies[4 + n].wait_recv()
        to_sibling(5 + n, (1 - x_hi) * 4 + lax.rem(z + 4 - i, 4))

    loads[0].wait_recv()
    for cp in sib_copies:
        cp.wait_recv()
    r2_copies = [None]
    for i in list(range(1, 8)) + [0]:
        dst = lax.rem(t + i, 8)
        for e in range(2):
            part = dot(inner[...], wd_all[dst * 2 + e])
            if i == 0:
                own_part2[:, e * 512 : (e + 1) * 512] = part
            else:
                rs2_send[i, :, e * 512 : (e + 1) * 512] = part.astype(BF)
        if i:
            r2_copies.append(
                remote(rs2_send.at[i], rs2_recv.at[i], r2_s.at[i], r2_r.at[i], tp_at(i))
            )

    for n in ("xyp", "xym", "g1", "g2"):
        txt[n].wait_recv()
    project_text(3, 7)
    project_text(4, 5)

    @pl.loop(0, 4)
    def _(r):
        sl = pl.ds(pl.multiple_of(r * 128, 128), 128)
        inv = inverse(ss_t[sl, :])
        q_text[sl, :] = (acc_t[sl, 0:512] * inv).astype(BF)
        kv_text[0, sl, :] = (acc_t[sl, 512:768] * inv).astype(BF)

    def kt_copy(j):
        return pltpu.make_async_remote_copy(
            src_ref=kv_text.at[0], dst_ref=kv_text.at[j], send_sem=kt_s.at[j], recv_sem=kt_r.at[j],
            device_id=ctx_at(j), device_id_type=MESH,
        )

    for j in range(1, 5):

        @pl.when(c + j < 8)
        def _():
            kt_copy(j).start()

    for cp in r2_copies[1:]:
        cp.wait_recv()
    total = own_part2[...]
    for i in range(1, 8):
        total += rs2_recv[i].astype(F32)
    vis_all[0] = total.astype(BF)
    vs_copies = [None]
    for i in range(1, 8):
        vs_copies.append(remote(vis_all.at[0], vis_all.at[i], vs_s.at[i], vs_r.at[i], tp_at(i)))

    for cp in vs_copies[1:]:
        cp.wait_recv()
    acc_v[...] = jnp.zeros_like(acc_v)
    ss_v[...] = jnp.zeros_like(ss_v)

    @pl.loop(0, 8)
    def _(slot):
        project(vis_all, slot, lax.rem(t + 8 - slot, 8), acc_v, ss_v, 128, 128)

    inv = inverse(ss_v[...])
    kv_own[...] = (acc_v[:, 512:768] * inv).astype(BF)
    kv_copies = []
    for i in range(1, 8):
        kv_copies.append(remote(kv_own, kv_vis.at[c], kv_s.at[i], kv_r.at[i], ctx_at(i)))
    kv_vis[c] = kv_own[...]
    qv = (acc_v[:, 0:512] * inv).astype(BF)
    dest = place_row[...] // 512
    hit = lax.broadcasted_iota(jnp.int32, (8, 128), 0) == dest
    hit_f = hit.astype(F32)
    before = (
        lax.broadcasted_iota(jnp.int32, (128, 128), 0) < lax.broadcasted_iota(jnp.int32, (128, 128), 1)
    ).astype(F32).astype(BF)
    rank = jnp.sum(dot(hit_f.astype(BF), before) * hit_f, axis=0, keepdims=True)
    slot_row = dest * 32 + rank.astype(jnp.int32)
    pick = (lax.broadcasted_iota(jnp.int32, (256, 128), 0) == slot_row).astype(F32).astype(BF)
    slots_out[...] = dot(pick, qv).astype(BF)
    qs_copies = []
    for i in range(1, 8):
        sl = pl.ds(pl.multiple_of(lax.rem(c + i, 8) * 32, 32), 32)
        qs_copies.append(remote(slots_out.at[sl], q_slots.at[c], qs_s.at[i], qs_r.at[i], ctx_at(i)))
    q_slots[c] = slots_out[pl.ds(pl.multiple_of(c * 32, 32), 32), :]

    for j in range(1, 5):

        @pl.when(c - j >= 0)
        def _():
            kt_copy(j).wait_recv()

        @pl.when(c + j < 8)
        def _():
            kt_copy(j).wait_send()

    finish()


def attend_kernel(
    q_text, kv_text, q_slots, kv_vis, pos_all, seg_s, segments, out,
    place, expand, q_v, k_v, v_v, m_v, l_v, acc,
):
    c = lax.axis_index("ctx")
    lanes = kv_vis.shape[1]
    own = pl.ds(pl.multiple_of(c * 512, 512), 512)
    pos = pos_all[...]
    hit = (pos // 512) == c
    before = (
        lax.broadcasted_iota(jnp.int32, (128, 128), 0) < lax.broadcasted_iota(jnp.int32, (128, 128), 1)
    ).astype(F32).astype(BF)
    rank = dot(hit.astype(F32).astype(BF), before).astype(jnp.int32)
    slot = jnp.where(hit, rank, -1)
    ones = jnp.ones((1024, 128), BF)

    for s in range(8):
        back = (lax.broadcasted_iota(jnp.int32, (32, lanes), 0) == slot[s : s + 1, :]).astype(F32)
        expand[s * lanes : (s + 1) * lanes, :] = dot(
            jnp.transpose(back).astype(BF), q_slots[s]
        ).astype(BF)
    seg_q = jnp.transpose(jnp.broadcast_to(segments[:, own], (8, 512)))[:, 0:1]
    log2e = 1.4426950408889634

    for j in range(5):
        base = (c - j) * 512
        first = jnp.maximum(base, 0)

        @pl.when((base >= 0) & (seg_s[0, first + 511] == seg_s[0, c * 512]) if j else base >= 0)
        def _():
            rows = lax.broadcasted_iota(jnp.int32, (512, lanes), 0) + base
            for s in range(8):
                place[:, s * lanes : (s + 1) * lanes] = (
                    (rows == pos[s : s + 1, :]).astype(F32).astype(BF)
                )
            is_vis = dot(place[...], ones) > 0.5
            placed = dot(place[...], kv_vis[...].reshape(1024, 256))
            k_v[...] = jnp.where(is_vis, placed[:, 0:128], kv_text[j, :, 0:128].astype(F32)).astype(BF)
            v_v[...] = jnp.where(is_vis, placed[:, 128:256], kv_text[j, :, 128:256].astype(F32)).astype(BF)
            if j == 0:
                placed_q = dot(place[...], expand[...])
                for h in range(4):
                    sl = slice(h * 128, (h + 1) * 128)
                    qh = jnp.where(is_vis, placed_q[:, sl], q_text[:, sl].astype(F32)).astype(BF)
                    for r in range(4):
                        q_v[r, sl, :] = qh[r * 128 : (r + 1) * 128, :]
            seg_k = segments[:, pl.ds(pl.multiple_of(first, 512), 512)]
            for r in range(4):
                wide = (r + 1) * 128 if j == 0 else 512
                allowed = seg_q[r * 128 : (r + 1) * 128] == seg_k[:, 0:wide]
                if j == 0:
                    allowed = allowed & (
                        lax.broadcasted_iota(jnp.int32, (128, wide), 1)
                        <= lax.broadcasted_iota(jnp.int32, (128, wide), 0) + r * 128
                    )
                bias = jnp.where(allowed, 0.0, MASKED)
                s_ = dot_nt(q_v[r], k_v[0:wide, :]) * (HD ** (-0.5) * log2e)
                s_ = (s_.reshape(4, 128, wide) + bias[None]).reshape(512, wide)
                top = jnp.max(s_, axis=-1, keepdims=True)
                if j == 0:
                    w = jnp.exp2(s_ - top)
                    m_v[r] = jnp.broadcast_to(top, (512, 128))
                    l_v[r] = jnp.broadcast_to(jnp.sum(w, axis=-1, keepdims=True), (512, 128))
                    acc[r] = dot(w.astype(BF), v_v[0:wide, :])
                else:
                    old = m_v[r]
                    new = jnp.maximum(old, top)
                    alpha = jnp.exp2(old - new)
                    w = jnp.exp2(s_ - new[:, 0:1])
                    m_v[r] = new
                    l_v[r] = l_v[r] * alpha + jnp.sum(w, axis=-1, keepdims=True)
                    acc[r] = acc[r] * alpha + dot(w.astype(BF), v_v[...])

    for r in range(4):
        for h in range(4):
            sl = slice(h * 128, (h + 1) * 128)
            out[r * 128 : (r + 1) * 128, sl] = (acc[r, sl, :] / l_v[r, sl, :]).astype(BF)


def shards(
    patches, window_ids, vit_gain, vit_qkv, vit_out, merge_gain, merge_up, merge_down,
    text_rows, placeholders, segments, llm_gain, w_query, w_keyval,
):
    vm = pl.BlockSpec(memory_space=pltpu.VMEM)
    hbm = pl.BlockSpec(memory_space=pl.ANY)
    dma = pltpu.SemaphoreType.DMA
    sds = jax.ShapeDtypeStruct
    qkv_t = vit_qkv.transpose(1, 2, 0).reshape(480, 1280)
    encoded = pl.pallas_call(
        encode_kernel,
        out_shape=(
            sds((512, 512), BF), sds((5, 512, 256), BF), sds((8, 32, 512), BF),
            sds((8, 128, 256), BF), sds((8, 128), jnp.int32),
        ),
        in_specs=[vm, vm, vm, vm, vm, vm, hbm, hbm, hbm, vm, vm, hbm, hbm],
        out_specs=(vm, vm, vm, vm, vm),
        scratch_shapes=[
            pltpu.VMEM((8, 512, 1024), BF),
            pltpu.VMEM((5120, 640), BF),
            pltpu.VMEM((16, 640, 512), BF),
            pltpu.VMEM((8192, 512), BF),
            pltpu.VMEM((2, 2048, 128), BF),
            pltpu.VMEM((2048, 128), F32),
            pltpu.VMEM((8192, 256), BF),
            pltpu.VMEM((512, 160), BF),
            pltpu.VMEM((512, 160), BF),
            pltpu.VMEM((512, 160), BF),
            pltpu.VMEM((512, 160), BF),
            pltpu.VMEM((8, 64, 1280), BF),
            pltpu.VMEM((8, 64, 1280), BF),
            pltpu.VMEM((64, 1280), F32),
            pltpu.VMEM((10, 64, 128), F32),
            pltpu.VMEM((128, 5120), BF),
            pltpu.VMEM((128, 640), F32),
            pltpu.VMEM((128, 640), BF),
            pltpu.VMEM((8, 128, 1024), BF),
            pltpu.VMEM((8, 128, 1024), BF),
            pltpu.VMEM((128, 1024), F32),
            pltpu.VMEM((8, 128, 1024), BF),
            pltpu.VMEM((512, 768), F32),
            pltpu.VMEM((512, 128), F32),
            pltpu.VMEM((128, 768), F32),
            pltpu.VMEM((128, 128), F32),
            pltpu.VMEM((256, 512), BF),
            pltpu.VMEM((128, 256), BF),
            dma((6,)), dma((9,)), dma((9,)),
        ] + [dma((8,))] * 20,
        compiler_params=pltpu.CompilerParams(
            collective_id=0, has_side_effects=True, vmem_limit_bytes=63 * 2**20
        ),
    )(
        patches[0], window_ids, vit_gain, qkv_t, vit_out,
        merge_gain, merge_up, merge_down, text_rows[0], placeholders,
        llm_gain, w_query, w_keyval.reshape(16384, 128),
    )
    out = pl.pallas_call(
        attend_kernel,
        out_shape=sds((512, 512), BF),
        in_specs=[vm] * 5 + [pl.BlockSpec(memory_space=pltpu.SMEM), vm],
        out_specs=vm,
        scratch_shapes=[
            pltpu.VMEM((512, 1024), BF),
            pltpu.VMEM((1024, 512), BF),
            pltpu.VMEM((4, 512, 128), BF),
            pltpu.VMEM((512, 128), BF),
            pltpu.VMEM((512, 128), BF),
            pltpu.VMEM((4, 512, 128), F32),
            pltpu.VMEM((4, 512, 128), F32),
            pltpu.VMEM((4, 512, 128), F32),
        ],
        compiler_params=pltpu.CompilerParams(vmem_limit_bytes=60 * 2**20),
    )(*encoded, segments, segments)
    return out[None]


def solution(mesh):
    in_specs = (
        P("dp", "ctx", None),
        P("dp", "ctx"),
        P(),
        P(None, None, "tp"),
        P("tp", None),
        P(),
        P(None, "tp"),
        P("tp", ("ctx", "dp")),
        P("dp", "ctx", "tp"),
        P("dp", "ctx"),
        P("dp", None),
        P(),
        P(None, "tp"),
        P(None, None, "tp"),
    )
    out_specs = P("dp", "ctx", "tp")
    return jax.shard_map(shards, mesh=mesh, in_specs=in_specs, out_specs=out_specs, check_vma=False)
```

time: 308 us -> 214 us (0.69)
  the two profiles are of different devices: /device:TPU:6 before, /device:TPU:94 now
where the time goes in v2:
time: 214 us; the launch traced here: 213 us
  Pallas kernels  213 us (100%)
    pallas_call x1, Pallas kernels, shards(): pl.pallas_call(encode_kernel, out_shape=(sds((512, 512), BF), sds((5, 512...  192 us
    pallas_call x1, Pallas kernels, shards(): pl.pallas_call(attend_kernel, out_shape=sds((512, 512), BF), in_specs=[vm...  21.3 us

profile of v2, /device:TPU:94, one launch (start us, length us, event | category | flops | bytes accessed | tf_op | source)
XLA Modules:
  0.0 213.5 jit_solution(3269870291705380597)
XLA Ops:
  0.0 192.1 %shard_map.136 = (bf16[512,512]{1,0:T(8,128)(2,1)}, bf16[5,512,256]{2,1,0:T(8,128)(2,1)}, bf16[8,32,512]{2,1,0:T(8,128)(2,1)}, bf16[8,128,256]{2,1,0:T(8,128)(2,1)}, s32[8,128]{1,0:T(8,128)}) custom-call(bf16[512,1280]{1,0:T(8,128)(2,1)} %bitcast.8, s32[1,512]{1,0:T(1,128)} %window_row.1, f32[1280]{0:T(1024)} %vit_gain.1, bf16[480,1280]{1,0:T(8,128)(2,1)} %bitcast.9, ...), custom_call_target="tpu_custom_call" | custom-call | tf_op jit(solution)/shard_map/pallas_call | solution.py:465
  192.2 21.3 %shard_map.137 = bf16[512,512]{1,0:T(8,128)(2,1)} custom-call(bf16[512,512]{1,0:T(8,128)(2,1)} %get-tuple-element.10.q_text, bf16[5,512,256]{2,1,0:T(8,128)(2,1)} %get-tuple-element.11.kv_text, bf16[8,32,512]{2,1,0:T(8,128)(2,1)} %get-tuple-element.12.q_slots, bf16[8,128,256]{2,1,0:T(8,128)(2,1)} %get-tuple-element.13.kv_vis, ...), custom_call_target="tpu_custom_call" | custom-call | tf_op jit(solution)/shard_map/pallas_call | solution.py:512

commit v3 on v2

--- a/solution.py
+++ b/solution.py
@@ -205,11 +205,31 @@
         for b in range(10):
             at = j * 1280 + b * 128
             merged[own_m, at : at + 128] = merge_f[b, pl.ds(j, 16, stride=4), :].astype(BF)
-    mg_copies = []
-    for i in range(1, 8):
-        mg_copies.append(
-            remote(merged.at[own_m], merged.at[own_m], mg_s.at[i], mg_r.at[i], tp_at(i))
-        )
+    def merged_at(dy, dx, cols=slice(None)):
+        block = lax.rem(y + dy, 4) * 2 + lax.rem(x + dx, 2)
+        return merged.at[pl.ds(pl.multiple_of(block * 16, 16), 16), cols]
+
+    mrg = {}
+
+    def merged_send(name, ref, dev):
+        n = len(mrg)
+        mrg[name] = remote(ref, ref, mg_s.at[n], mg_r.at[n], dev)
+
+    left, right = pl.ds(0, 2560), pl.ds(2560, 2560)
+    merged_send("yp", merged_at(0, 0), grid_at(1, 0))
+    merged_send("ym", merged_at(0, 0), grid_at(3, 0))
+    merged_send("x0", merged_at(0, 0), grid_at(0, 1))
+    mrg["yp"].wait_recv()
+    merged_send("f1", merged_at(3, 0, left), grid_at(1, 0))
+    mrg["ym"].wait_recv()
+    merged_send("f2", merged_at(1, 0, right), grid_at(3, 0))
+    mrg["x0"].wait_recv()
+    merged_send("xyp", merged_at(0, 1), grid_at(1, 0))
+    merged_send("xym", merged_at(0, 1), grid_at(3, 0))
+    mrg["f1"].wait_recv()
+    merged_send("g1", merged_at(2, 0, left), grid_at(0, 1))
+    mrg["f2"].wait_recv()
+    merged_send("g2", merged_at(2, 0, right), grid_at(0, 1))
 
     loads[2].wait_recv()
     loads[3].wait_recv()
@@ -245,16 +265,12 @@
     txt["x0"].wait_recv()
     project_text(0, 1)
 
-    for cp in mg_copies:
+    for cp in mrg.values():
         cp.wait_recv()
     txt["yp"].wait_recv()
     text_send("f1", slot_of(3, 0).at[lo], slot_of(2, 0).at[lo], grid_at(1, 0))
     txt["ym"].wait_recv()
     text_send("f2", slot_of(1, 0).at[hi], slot_of(2, 0).at[hi], grid_at(3, 0))
-    txt["x0"].wait_recv()
-    text_send("xyp", slot_of(0, 1), slot_of(3, 1), grid_at(1, 0))
-    text_send("xym", slot_of(0, 1), slot_of(1, 1), grid_at(3, 0))
-
     loads[1].wait_recv()
     acc_up[...] = jnp.zeros_like(acc_up)
 
@@ -269,8 +285,8 @@
     project_text(2, 6)
     txt["f1"].wait_recv()
     text_send("g1", slot_of(2, 0).at[lo], slot_of(2, 1).at[lo], grid_at(0, 1))
-    txt["f2"].wait_recv()
-    text_send("g2", slot_of(2, 0).at[hi], slot_of(2, 1).at[hi], grid_at(0, 1))
+    text_send("xyp", slot_of(0, 1), slot_of(3, 1), grid_at(1, 0))
+    text_send("xym", slot_of(0, 1), slot_of(1, 1), grid_at(3, 0))
     for n, i in enumerate((1, 3, 2)):
         wd_copies[1 + n].wait_recv()
         to_sibling(2 + n, x_hi * 4 + lax.rem(z + 4 - i, 4))
@@ -281,23 +297,63 @@
     loads[0].wait_recv()
     for cp in sib_copies:
         cp.wait_recv()
-    r2_copies = [None]
-    for i in list(range(1, 8)) + [0]:
-        dst = lax.rem(t + i, 8)
+    def partial(dy, dx, e):
+        block = lax.rem(y + dy, 4) * 2 + lax.rem(x + dx, 2)
+        return dot(inner[...], wd_all[block * 2 + e])
+
+    def make(dy, dx):
         for e in range(2):
-            part = dot(inner[...], wd_all[dst * 2 + e])
-            if i == 0:
-                own_part2[:, e * 512 : (e + 1) * 512] = part
-            else:
-                rs2_send[i, :, e * 512 : (e + 1) * 512] = part.astype(BF)
-        if i:
-            r2_copies.append(
-                remote(rs2_send.at[i], rs2_recv.at[i], r2_s.at[i], r2_r.at[i], tp_at(i))
-            )
-
-    for n in ("xyp", "xym", "g1", "g2"):
+            rs2_send[dy * 2 + dx, :, e * 512 : (e + 1) * 512] = partial(dy, dx, e).astype(BF)
+
+    sums = []
+
+    def sum_send(src, dst, dev):
+        n = len(sums)
+        sums.append(remote(src, dst, r2_s.at[n], r2_r.at[n], dev))
+
+    def add(slot, part, rows):
+        rs2_send[slot, rows, :] = (
+            rs2_send[slot, rows, :].astype(F32) + rs2_recv[part, rows, :].astype(F32)
+        ).astype(BF)
+
+    top, low = pl.ds(0, 64), pl.ds(64, 64)
+    every = pl.ds(0, 128)
+    make(2, 1)
+    sum_send(rs2_send.at[5], rs2_recv.at[0], grid_at(0, 1))
+    make(1, 1)
+    sum_send(rs2_send.at[3], rs2_recv.at[1], grid_at(1, 0))
+    make(3, 1)
+    sum_send(rs2_send.at[7], rs2_recv.at[2], grid_at(3, 0))
+    make(2, 0)
+    make(0, 1)
+    make(1, 0)
+    make(3, 0)
+    for e in range(2):
+        own_part2[:, e * 512 : (e + 1) * 512] = partial(0, 0, e)
+    sums[0].wait_recv()
+    add(4, 0, every)
+    sum_send(rs2_send.at[4, top], rs2_recv.at[3, top], grid_at(1, 0))
+    sum_send(rs2_send.at[4, low], rs2_recv.at[3, low], grid_at(3, 0))
+    sums[1].wait_recv()
+    sums[2].wait_recv()
+    add(1, 1, every)
+    add(1, 2, every)
+    sum_send(rs2_send.at[1], rs2_recv.at[4], grid_at(0, 1))
+    sums[3].wait_recv()
+    add(2, 3, top)
+    sum_send(rs2_send.at[2], rs2_recv.at[5], grid_at(1, 0))
+    sums[4].wait_recv()
+    add(6, 3, low)
+    sum_send(rs2_send.at[6], rs2_recv.at[6], grid_at(3, 0))
+
+    third, last = pl.ds(256, 128), pl.ds(384, 128)
+    txt["xyp"].wait_recv()
+    text_send("h1", slot_of(3, 1).at[third], slot_of(2, 1).at[third], grid_at(1, 0))
+    txt["xym"].wait_recv()
+    text_send("h2", slot_of(1, 1).at[last], slot_of(2, 1).at[last], grid_at(3, 0))
+    project_text(3, 7)
+    for n in ("f2", "g1", "h1", "h2"):
         txt[n].wait_recv()
-    project_text(3, 7)
     project_text(4, 5)
 
     @pl.loop(0, 4)
@@ -307,36 +363,76 @@
         q_text[sl, :] = (acc_t[sl, 0:512] * inv).astype(BF)
         kv_text[0, sl, :] = (acc_t[sl, 512:768] * inv).astype(BF)
 
-    def kt_copy(j):
+    def kt_copy(src, dst, n, dev):
         return pltpu.make_async_remote_copy(
-            src_ref=kv_text.at[0], dst_ref=kv_text.at[j], send_sem=kt_s.at[j], recv_sem=kt_r.at[j],
-            device_id=ctx_at(j), device_id_type=MESH,
+            src_ref=kv_text.at[src], dst_ref=kv_text.at[dst], send_sem=kt_s.at[n], recv_sem=kt_r.at[n],
+            device_id=dev, device_id_type=MESH,
         )
 
-    for j in range(1, 5):
-
-        @pl.when(c + j < 8)
+    def kt_along(i):
+        return kt_copy(0, i, i, z_at(i))
+
+    def kt_on(i):
+        return kt_copy(4, 4 - i, 4 + i, z_at(4 - i))
+
+    kt_cross = kt_copy(0, 4, 4, (partner, t, d))
+
+    @pl.when(x_hi == 0)
+    def _():
+        kt_cross.start()
+
+    for i in range(1, 4):
+
+        @pl.when(z + i < 4)
         def _():
-            kt_copy(j).start()
-
-    for cp in r2_copies[1:]:
+            kt_along(i).start()
+
+    for cp in sums:
         cp.wait_recv()
     total = own_part2[...]
-    for i in range(1, 8):
+    for i in range(4, 7):
         total += rs2_recv[i].astype(F32)
     vis_all[0] = total.astype(BF)
-    vs_copies = [None]
-    for i in range(1, 8):
-        vs_copies.append(remote(vis_all.at[0], vis_all.at[i], vs_s.at[i], vs_r.at[i], tp_at(i)))
-
-    for cp in vs_copies[1:]:
+    vis_at = lambda dy, dx: vis_all.at[dy * 2 + dx]
+    vis = {}
+
+    def vis_send(name, src, dst, dev):
+        n = len(vis)
+        vis[name] = remote(src, dst, vs_s.at[n], vs_r.at[n], dev)
+
+    vis_send("yp", vis_at(0, 0), vis_at(3, 0), grid_at(1, 0))
+    vis_send("ym", vis_at(0, 0), vis_at(1, 0), grid_at(3, 0))
+    vis_send("x0", vis_at(0, 0), vis_at(0, 1), grid_at(0, 1))
+    vis["yp"].wait_recv()
+    vis_send("f1", vis_at(3, 0).at[top], vis_at(2, 0).at[top], grid_at(1, 0))
+    vis["ym"].wait_recv()
+    vis_send("f2", vis_at(1, 0).at[low], vis_at(2, 0).at[low], grid_at(3, 0))
+    vis["x0"].wait_recv()
+    vis_send("xyp", vis_at(0, 1), vis_at(3, 1), grid_at(1, 0))
+    vis_send("xym", vis_at(0, 1), vis_at(1, 1), grid_at(3, 0))
+    vis["f1"].wait_recv()
+    vis_send("g1", vis_at(2, 0).at[top], vis_at(2, 1).at[top], grid_at(0, 1))
+    vis["f2"].wait_recv()
+    vis_send("g2", vis_at(2, 0).at[low], vis_at(2, 1).at[low], grid_at(0, 1))
+
+    @pl.when(x_hi == 1)
+    def _():
+        kt_cross.wait_recv()
+        for i in range(1, 4):
+
+            @pl.when(z - i >= 0)
+            def _():
+                kt_on(i).start()
+
+    for cp in vis.values():
         cp.wait_recv()
     acc_v[...] = jnp.zeros_like(acc_v)
     ss_v[...] = jnp.zeros_like(ss_v)
 
     @pl.loop(0, 8)
     def _(slot):
-        project(vis_all, slot, lax.rem(t + 8 - slot, 8), acc_v, ss_v, 128, 128)
+        block = lax.rem(y + slot // 2, 4) * 2 + lax.rem(x + lax.rem(slot, 2), 2)
+        project(vis_all, slot, block, acc_v, ss_v, 128, 128)
 
     inv = inverse(ss_v[...])
     kv_own[...] = (acc_v[:, 512:768] * inv).astype(BF)
@@ -361,15 +457,27 @@
         qs_copies.append(remote(slots_out.at[sl], q_slots.at[c], qs_s.at[i], qs_r.at[i], ctx_at(i)))
     q_slots[c] = slots_out[pl.ds(pl.multiple_of(c * 32, 32), 32), :]
 
-    for j in range(1, 5):
-
-        @pl.when(c - j >= 0)
+    @pl.when(x_hi == 0)
+    def _():
+        kt_cross.wait_send()
+
+    for i in range(1, 4):
+
+        @pl.when(z - i >= 0)
         def _():
-            kt_copy(j).wait_recv()
-
-        @pl.when(c + j < 8)
+            kt_along(i).wait_recv()
+
+        @pl.when(z + i < 4)
         def _():
-            kt_copy(j).wait_send()
+            kt_along(i).wait_send()
+
+        @pl.when((x_hi == 1) & (z + i < 4))
+        def _():
+            kt_on(i).wait_recv()
+
+        @pl.when((x_hi == 1) & (z - i >= 0))
+        def _():
+            kt_on(i).wait_send()
 
     finish()
 
@@ -499,8 +607,8 @@
             pltpu.VMEM((128, 128), F32),
             pltpu.VMEM((256, 512), BF),
             pltpu.VMEM((128, 256), BF),
-            dma((6,)), dma((9,)), dma((9,)),
-        ] + [dma((8,))] * 20,
+            dma((6,)), dma((10,)), dma((10,)),
+        ] + [dma((9,))] * 20,
         compiler_params=pltpu.CompilerParams(
             collective_id=0, has_side_effects=True, vmem_limit_bytes=63 * 2**20
         ),

time: 214 us -> 182 us (0.85)
  the two profiles are of different devices: /device:TPU:94 before, /device:TPU:96 now
where the time goes in v3:
time: 182 us
  Pallas kernels  182 us (100%)
    pallas_call x1, Pallas kernels, shards(): pl.pallas_call(encode_kernel, out_shape=(sds((512, 512), BF), sds((5, 512...  165 us
    pallas_call x1, Pallas kernels, shards(): pl.pallas_call(attend_kernel, out_shape=sds((512, 512), BF), in_specs=[vm...  17.6 us

profile of v3, /device:TPU:96, one launch (start us, length us, event | category | flops | bytes accessed | tf_op | source)
XLA Modules:
  0.0 182.2 jit_solution(10304684296184402506)
XLA Ops:
  0.0 164.6 %shard_map.136 = (bf16[512,512]{1,0:T(8,128)(2,1)}, bf16[5,512,256]{2,1,0:T(8,128)(2,1)}, bf16[8,32,512]{2,1,0:T(8,128)(2,1)}, bf16[8,128,256]{2,1,0:T(8,128)(2,1)}, s32[8,128]{1,0:T(8,128)}) custom-call(bf16[512,1280]{1,0:T(8,128)(2,1)} %bitcast.8, s32[1,512]{1,0:T(1,128)} %window_row.1, f32[1280]{0:T(1024)} %vit_gain.1, bf16[480,1280]{1,0:T(8,128)(2,1)} %bitcast.9, ...), custom_call_target="tpu_custom_call" | custom-call | tf_op jit(solution)/shard_map/pallas_call | solution.py:573
  164.6 17.6 %shard_map.137 = bf16[512,512]{1,0:T(8,128)(2,1)} custom-call(bf16[512,512]{1,0:T(8,128)(2,1)} %get-tuple-element.10.q_text, bf16[5,512,256]{2,1,0:T(8,128)(2,1)} %get-tuple-element.11.kv_text, bf16[8,32,512]{2,1,0:T(8,128)(2,1)} %get-tuple-element.12.q_slots, bf16[8,128,256]{2,1,0:T(8,128)(2,1)} %get-tuple-element.13.kv_vis, ...), custom_call_target="tpu_custom_call" | custom-call | tf_op jit(solution)/shard_map/pallas_call | solution.py:620

commit v4 on v3

--- a/solution.py
+++ b/solution.py
@@ -529,7 +529,7 @@
                     for r in range(4):
                         q_v[r, sl, :] = qh[r * 128 : (r + 1) * 128, :]
             seg_k = segments[:, pl.ds(pl.multiple_of(first, 512), 512)]
-            for r in range(4):
+            def rows_of(r):
                 wide = (r + 1) * 128 if j == 0 else 512
                 allowed = seg_q[r * 128 : (r + 1) * 128] == seg_k[:, 0:wide]
                 if j == 0:
@@ -554,6 +554,12 @@
                     m_v[r] = new
                     l_v[r] = l_v[r] * alpha + jnp.sum(w, axis=-1, keepdims=True)
                     acc[r] = acc[r] * alpha + dot(w.astype(BF), v_v[...])
+
+            for r in range(4):
+                if j == 0:
+                    rows_of(r)
+                else:
+                    pl.when(seg_s[0, first + 511] == seg_s[0, c * 512 + r * 128])(lambda r=r: rows_of(r))
 
     for r in range(4):
         for h in range(4):

time: 182 us -> 182 us (level)
  no operation moved by 1% of the time
where the time goes in v4:
time: 182 us
  Pallas kernels  182 us (100%)
    pallas_call x1, Pallas kernels, shards(): pl.pallas_call(encode_kernel, out_shape=(sds((512, 512), BF), sds((5, 512...  165 us
    pallas_call x1, Pallas kernels, shards(): pl.pallas_call(attend_kernel, out_shape=sds((512, 512), BF), in_specs=[vm...  17.1 us

profile of v4, /device:TPU:96, one launch (start us, length us, event | category | flops | bytes accessed | tf_op | source)
XLA Modules:
  0.0 181.7 jit_solution(13703338092386814057)
XLA Ops:
  0.0 164.6 %shard_map.136 = (bf16[512,512]{1,0:T(8,128)(2,1)}, bf16[5,512,256]{2,1,0:T(8,128)(2,1)}, bf16[8,32,512]{2,1,0:T(8,128)(2,1)}, bf16[8,128,256]{2,1,0:T(8,128)(2,1)}, s32[8,128]{1,0:T(8,128)}) custom-call(bf16[512,1280]{1,0:T(8,128)(2,1)} %bitcast.8, s32[1,512]{1,0:T(1,128)} %window_row.1, f32[1280]{0:T(1024)} %vit_gain.1, bf16[480,1280]{1,0:T(8,128)(2,1)} %bitcast.9, ...), custom_call_target="tpu_custom_call" | custom-call | tf_op jit(solution)/shard_map/pallas_call | solution.py:579
  164.6 17.1 %shard_map.137 = bf16[512,512]{1,0:T(8,128)(2,1)} custom-call(bf16[512,512]{1,0:T(8,128)(2,1)} %get-tuple-element.10.q_text, bf16[5,512,256]{2,1,0:T(8,128)(2,1)} %get-tuple-element.11.kv_text, bf16[8,32,512]{2,1,0:T(8,128)(2,1)} %get-tuple-element.12.q_slots, bf16[8,128,256]{2,1,0:T(8,128)(2,1)} %get-tuple-element.13.kv_vis, ...), custom_call_target="tpu_custom_call" | custom-call | tf_op jit(solution)/shard_map/pallas_call | solution.py:626
